TPU v7x, 32 devices: a whole 2x2x4 slice. The times are simulated.
32 devices in a mesh: pair: 8 (over z, y), rep: 4 (over x, core).
Axes of the slice: x: 2, y: 2, z: 4, core: 2. Of those that a mesh axis runs over, the one named last changes fastest.
Arguments:
- tau_ao: bfloat16 [512, 8192], P('pair'), may hold values from -6 to 6
- slab_sizes: int32 [32], replicated, may hold values from 1 to 512, 8192 in all
- integrals: bfloat16 [32, 512, 1024], P('pair', 'rep'), may hold values from -0.0625 to 0.0625
- transform: float32 [1024, 512], replicated, may hold values from -0.1875 to 0.1875
Outputs:
- ladder_mo: float32 [512, 512], P('pair', 'rep')
Inputs may be any that keep to these rules, and one draw needn't show every extreme that they name: `slab_sizes`: the sizes sum to 8192 and the largest equals 512.
All inputs are finite; a program needn't handle non-finite values.
Results may differ from a plain program's by a relative error of at most 0.0003.
Values may be sent and summed in bfloat16 or wider, within the bound.
A program may use at most 128 MiB of HBM per device.

v0:
```python
import jax
import jax.numpy as jnp
from jax import lax
from jax.sharding import PartitionSpec as P


def pick_columns(tau_rows, offsets, sizes_int, slot_index):
    packed_cols = tau_rows.shape[1]
    columns = jnp.clip(offsets[:, None] + slot_index[None, :], 0, packed_cols - 1)
    filled = (slot_index[None, :] < sizes_int[:, None]).reshape(-1)
    picked = jnp.take(tau_rows, columns.reshape(-1), axis=1)
    return jnp.where(filled[None, :], picked, jnp.zeros_like(picked))


def regroup(picked, pair_count, width):
    outgoing = picked.reshape(picked.shape[0], pair_count, width)
    arrived = lax.all_to_all(outgoing, "pair", split_axis=1, concat_axis=0, tiled=True)
    return arrived.reshape(pair_count * picked.shape[0], width)


def contract(pair_amps, slab_weights, transform):
    partial_ao = lax.psum_scatter(
        jnp.dot(pair_amps, slab_weights, preferred_element_type=jnp.float32),
        "pair",
        scatter_dimension=0,
        tiled=True,
    )
    return jnp.dot(partial_ao, transform, precision=lax.Precision.HIGHEST)


def body(tau_ao, slab_sizes, integrals, transform):
    pair_count = lax.axis_size("pair")
    rep_index = lax.axis_index("rep")
    slabs_here, slab_rows, out_width = integrals.shape
    offsets = jnp.cumsum(slab_sizes) - slab_sizes
    slot_index = rep_index * slab_rows + jnp.arange(slab_rows, dtype=jnp.int32)
    picked = pick_columns(tau_ao, offsets, slab_sizes, slot_index)
    pair_amps = regroup(picked, pair_count, slabs_here * slab_rows)
    slab_weights = integrals.reshape(slabs_here * slab_rows, out_width)
    forward = contract(pair_amps, slab_weights, transform)
    return lax.psum_scatter(forward, "rep", scatter_dimension=1, tiled=True)


def solution(mesh):
    return jax.shard_map(
        body,
        mesh=mesh,
        in_specs=(P("pair", None), P(), P("pair", "rep", None), P()),
        out_specs=P("pair", "rep"),
        check_vma=False,
    )
```

profile of v0, /device:TPU:0, one launch (start us, length us, event | category | flops | bytes accessed | tf_op | source)
XLA Modules:
  0.0 147.2 jit_solution(14880604081785408729)
XLA Ops:
  6.5 0.0 copy-start
  6.5 0.0 reduce-scatter.3.cloned.1.call-start
  6.5 0.9 lt.48
  7.4 0.7 copy.10
  8.2 0.1 reduce-window.9
  8.2 0.1 reduce
  8.3 0.7 sub.3
  9.0 0.1 add_clamp_fusion
  9.1 0.1 add.69
  9.2 2.8 %copy.12 = bf16[64,8192]{0,1:T(8,128)(2,1)} copy(bf16[64,8192]{1,0:T(8,128)(2,1)} %param.4) | data formatting | bytes 2097152 | tf_op args[0]
  12.0 12.9 %gather_fusion = bf16[4096,64]{1,0:T(8,128)(2,1)S(1)} fusion(bf16[64,8192]{0,1:T(8,128)(2,1)} %copy.12, s32[4096]{0:T(1024)S(1)} %broadcast_clamp_fusion), kind=kCustom, calls=%fused_computation | custom fusion | bytes 1064960 | tf_op jit(solution)/shard_map/jit(_take)/gather | solution.py:11
  24.9 1.1 copy.13
  26.0 0.0 copy-start.1
  26.0 0.1 copy.9
  26.1 0.1 copy.11
  26.2 0.1 bitcast_compare_fusion
  26.2 1.2 select_select_fusion
  27.4 21.6 %all_to_all.15 = bf16[64,8,512]{2,0,1:T(8,128)(2,1)S(1)} all-to-all(bf16[64,8,512]{2,0,1:T(8,128)(2,1)S(1)} %select_select_fusion), channel_id=1, replica_groups=mesh['pair'=8,'rep'=4] {'pair'}, dimensions={1} | all-to-all | bytes 1048576 | tf_op jit(solution)/shard_map/all_to_all | solution.py:17
  49.0 0.0 copy-done.1
  49.0 2.1 %fusion.4 = f32[512,1024]{1,0:T(8,128)} fusion(bf16[512,512]{1,0:T(8,128)(2,1)S(1)} %bitcast.35, bf16[512,1024]{1,0:T(8,128)(2,1)S(1)} %bitcast.36), kind=kOutput, calls=%fused_computation.14 | convolution fusion | flops 536870912 | bytes 3670016 | tf_op jit(solution)/shard_map/dot_general | solution.py:23
  51.1 0.0 reduce-scatter.3.cloned.1.call-update
  51.1 0.0 reduce-scatter.5.cloned.1.call-start
  51.2 67.4 %reduce-scatter.3.cloned.1.call-done = f32[64,1024]{1,0:T(8,128)} async-done(((f32[512,1024]{1,0:T(8,128)}), f32[64,1024]{1,0:T(8,128)}) %reduce-scatter.3.cloned.1.call-update) | async-done | bytes 262160 | tf_op jit(solution)/shard_map/reduce_scatter | solution.py:22
  118.6 0.0 copy-done
  118.6 3.0 %fusion.5 = f32[64,512]{1,0:T(8,128)} fusion(f32[64,1024]{1,0:T(8,128)} %reduce-scatter.3.cloned.1.call-done, f32[1024,512]{1,0:T(8,128)S(1)} %copy-done), kind=kOutput, calls=%fused_computation.15 | convolution fusion | flops 402653184 | bytes 2490368 | tf_op jit(solution)/shard_map/dot_general | solution.py:28
  121.6 0.0 reduce-scatter.5.cloned.1.call-update
  121.6 18.7 %reduce-scatter.5.cloned.1.call-done = f32[64,128]{1,0:T(8,128)} async-done(((f32[64,512]{1,0:T(8,128)}), f32[64,128]{1,0:T(8,128)}) %reduce-scatter.5.cloned.1.call-update) | async-done | bytes 32784 | tf_op jit(solution)/shard_map/reduce_scatter | solution.py:41
  (4 shorter events, 0.0 us)
Async XLA Ops:
  6.5 112.1 %copy-start = (f32[1024,512]{1,0:T(8,128)S(1)}, f32[1024,512]{1,0:T(8,128)}, u32[]{:S(2)}) copy-start(f32[1024,512]{1,0:T(8,128)} %param.7) | copy-start | bytes 6291460
  6.5 112.1 %reduce-scatter.3.cloned.1.call-start = ((), (), s32[]{:S(2)}) async-start(), calls=%async_computation.3 | async-start | bytes 2359296 | tf_op jit(solution)/shard_map/reduce_scatter | solution.py:22
  26.0 23.1 %copy-start.1 = (bf16[4,128,1024]{2,1,0:T(8,128)(2,1)S(1)}, bf16[4,128,1024]{2,1,0:T(8,128)(2,1)}, u32[]{:S(2)}) copy-start(bf16[4,128,1024]{2,1,0:T(8,128)(2,1)} %param.6) | copy-start | bytes 3145732
  51.1 89.2 %reduce-scatter.5.cloned.1.call-start = ((), (), s32[]{:S(2)}) async-start(), calls=%async_computation.4 | async-start | bytes 163840 | tf_op jit(solution)/shard_map/reduce_scatter | solution.py:41
Sparse Core Ops, SparseCore 0:
  51.3 67.3 reduce-scatter.2
  121.7 18.5 reduce-scatter.4
where the time goes:
time: 147 us
  waiting for transfers between devices  86.2 us (59%)
  blocking collectives  21.6 us (15%)
  local copies, waits for them, and re-layouts  18.7 us (13%)
  between operations  13.4 us (9%)
  matrix products  5.02 us (3%)
  other arithmetic  2.19 us (1%)
    reduce_scatter x1, waiting for transfers between devices, contract(): lax.psum_scatter(jnp.dot(pair_amps, slab_weights, preferred_element_type=...  67.4 us
    all_to_all x1, blocking collectives, regroup(): lax.all_to_all(outgoing, 'pair', split_axis=1, concat_axis=0, tiled=True)  21.6 us
    reduce_scatter x1, waiting for transfers between devices, body(): return lax.psum_scatter(forward, 'rep', scatter_dimension=1, tiled=True)  18.7 us
    gather x2, local copies, waits for them, and re-layouts, pick_columns(): picked = jnp.take(tau_rows, columns.reshape(-1), axis=1)  14 us
    dot_general x1, matrix products, contract(): return jnp.dot(partial_ao, transform, precision=lax.Precision.HIGHEST)  2.96 us
  transfers between devices with their start and end apart: 2, of which 2 were waited for; matrix products, arithmetic and copies ran while one was open for 0% of the time, Pallas kernels for 0%

commit v1 on v0

v1 whole, which is shorter than its diff:
```python
import functools

import jax
import jax.numpy as jnp
from jax import lax
from jax.experimental import pallas as pl
from jax.experimental.pallas import tpu as pltpu
from jax.sharding import PartitionSpec as P

MESH = pl.DeviceIdType.MESH
LANES = 128


def hop(slot, n):
    u = slot - 1
    h, odd = lax.div(u + 1, 2), lax.rem(u, 2)
    return n // 2 + h * (2 * odd - 1)


def pick_kernel(n, slabs, sizes, tau, target, offsets):
    me, rep = lax.axis_index("pair"), lax.axis_index("rep")
    pairs, packed = tau.shape
    rows = target.shape[2] // slabs

    def add_up(s, total):
        offsets[s] = total
        return total + sizes[s]

    lax.fori_loop(0, sizes.shape[0], add_up, jnp.int32(0))
    places = lax.broadcasted_iota(jnp.int32, (pairs, rows), 1) + rep * rows

    @pl.loop(0, n)
    def _(slot):
        dest = jnp.where(slot == 0, me, lax.rem(me + hop(slot, n), n))
        for q in range(slabs):
            slab = dest * slabs + q
            start = jnp.minimum(offsets[slab] + rep * rows, packed - 1)
            base = jnp.minimum(lax.div(start, LANES) * LANES, packed - 2 * LANES)
            window = tau[:, pl.ds(pl.multiple_of(base, LANES), 2 * LANES)].astype(jnp.float32)
            turned = pltpu.roll(window, 2 * LANES - (start - base), 1)[:, :rows]
            kept = jnp.where(places < sizes[slab], turned, 0.0)
            target[slot, :, q * rows : (q + 1) * rows] = kept.astype(jnp.bfloat16)


def kernel(
    n, amps_out, integrals_in, transform_in, out,
    integrals, transform, t_hi, t_lo, w_hi, w_lo, amps, part, core_in, x_in, done, back,
    load_sem, amps_send, amps_recv, core_send, core_recv, x_send, x_recv, back_send, back_recv,
):
    me, rep = lax.axis_index("pair"), lax.axis_index("rep")
    hi, lo = lax.div(rep, 2), lax.rem(rep, 2)
    near, far = hi * 2 + (1 - lo), (1 - hi) * 2 + lo
    slabs, rows, width = integrals.shape

    load_own = pltpu.make_async_copy(amps_out.at[0], amps.at[0], load_sem.at[0])
    load_integrals = pltpu.make_async_copy(integrals_in, integrals, load_sem.at[1])
    load_transform = pltpu.make_async_copy(transform_in, transform, load_sem.at[2])
    load_own.start()
    load_transform.start()
    load_integrals.start()

    barrier = pltpu.get_barrier_semaphore()

    @pl.loop(1, n)
    def _(slot):
        other = lax.rem(me + hop(slot, n), n)
        pl.semaphore_signal(barrier, inc=1, device_id=(other, rep), device_id_type=MESH)

    pl.semaphore_signal(barrier, inc=1, device_id=(me, near), device_id_type=MESH)
    pl.semaphore_signal(barrier, inc=1, device_id=(me, far), device_id_type=MESH)

    def send_amps(slot):
        other = lax.rem(me + hop(slot, n), n)
        return pltpu.make_async_remote_copy(
            src_ref=amps_out.at[slot], dst_ref=amps.at[slot],
            send_sem=amps_send.at[slot], recv_sem=amps_recv.at[slot],
            device_id=(other, rep), device_id_type=MESH,
        )

    def send_core(slot):
        return pltpu.make_async_remote_copy(
            src_ref=part.at[slot, 1 - lo], dst_ref=core_in.at[slot],
            send_sem=core_send.at[slot], recv_sem=core_recv.at[slot],
            device_id=(me, near), device_id_type=MESH,
        )

    def send_x(slot):
        return pltpu.make_async_remote_copy(
            src_ref=part.at[slot, lo, 1 - hi], dst_ref=x_in.at[slot],
            send_sem=x_send.at[slot], recv_sem=x_recv.at[slot],
            device_id=(me, far), device_id_type=MESH,
        )

    def send_back(slot):
        owner = lax.rem(me + n - hop(slot, n), n)
        return pltpu.make_async_remote_copy(
            src_ref=done.at[slot], dst_ref=back.at[slot],
            send_sem=back_send.at[slot], recv_sem=back_recv.at[slot],
            device_id=(owner, rep), device_id_type=MESH,
        )

    pl.semaphore_wait(barrier, n + 1)

    @pl.loop(1, n)
    def _(slot):
        send_amps(slot).start()

    load_transform.wait()

    @pl.loop(0, width, step=256)
    def _(k):
        block = transform[pl.ds(k, 256), :]
        high = block.astype(jnp.bfloat16)
        t_hi[pl.ds(k, 256), :] = high
        t_lo[pl.ds(k, 256), :] = (block - high.astype(jnp.float32)).astype(jnp.bfloat16)

    load_integrals.wait()
    for at in range(0, t_hi.shape[1], 2 * LANES):
        flat = integrals[...].reshape(slabs * rows, width)
        columns = slice(at, at + 2 * LANES)
        w = jnp.dot(flat, t_lo[:, columns], preferred_element_type=jnp.float32)
        w += jnp.dot(flat, t_hi[:, columns], preferred_element_type=jnp.float32)
        high = w.astype(jnp.bfloat16)
        w_hi[:, columns] = high
        w_lo[:, columns] = (w - high.astype(jnp.float32)).astype(jnp.bfloat16)

    load_own.wait()

    @pl.loop(0, n + 2)
    def _(step):
        @pl.when(jnp.logical_and(step >= 1, step < n))
        def _():
            send_amps(step).wait_recv()

        @pl.when(step < n)
        def _():
            block = amps[step]
            for h in range(2):
                columns = slice(h * 2 * LANES, (h + 1) * 2 * LANES)
                p = jnp.dot(block, w_lo[:, columns], preferred_element_type=jnp.float32)
                p += jnp.dot(block, w_hi[:, columns], preferred_element_type=jnp.float32)
                part[step, 0, h] = p[:, :LANES]
                part[step, 1, h] = p[:, LANES:]
            send_core(step).start()

        @pl.when(jnp.logical_and(step >= 1, step <= n))
        def _():
            slot = step - 1
            send_core(slot).wait_recv()
            part[slot, lo, 1 - hi] = part[slot, lo, 1 - hi] + core_in[slot, 1 - hi]
            send_x(slot).start()

        @pl.when(step >= 2)
        def _():
            slot = step - 2
            send_x(slot).wait_recv()
            done[slot] = part[slot, lo, hi] + core_in[slot, hi] + x_in[slot]

            @pl.when(slot >= 1)
            def _():
                send_back(slot).start()

    out[...] = done[0]

    @pl.loop(1, n)
    def _(slot):
        send_back(slot).wait_recv()
        out[...] = out[...] + back[slot]

    @pl.loop(0, n)
    def _(slot):
        @pl.when(slot >= 1)
        def _():
            send_amps(slot).wait_send()
            send_back(slot).wait_send()

        send_core(slot).wait_send()
        send_x(slot).wait_send()


def solution(mesh):
    n, reps = mesh.shape["pair"], mesh.shape["rep"]

    def body(tau_ao, slab_sizes, integrals, transform):
        pairs, packed = tau_ao.shape
        slabs, rows, width = integrals.shape
        virtuals = transform.shape[1]
        assert reps == 4 and rows == LANES and virtuals == reps * LANES
        slots = slabs * rows
        bf, f32, dma = jnp.bfloat16, jnp.float32, pltpu.SemaphoreType.DMA
        flops = 4 * slots * width * virtuals + 4 * n * pairs * slots * virtuals
        amps = pl.pallas_call(
            functools.partial(pick_kernel, n, slabs),
            out_shape=jax.ShapeDtypeStruct((n, pairs, slots), bf),
            in_specs=[
                pl.BlockSpec(memory_space=pltpu.SMEM),
                pl.BlockSpec(memory_space=pltpu.VMEM),
            ],
            out_specs=pl.BlockSpec(memory_space=pltpu.VMEM),
            scratch_shapes=[pltpu.SMEM((slab_sizes.shape[0],), jnp.int32)],
            compiler_params=pltpu.CompilerParams(vmem_limit_bytes=48 * 1024 * 1024),
            cost_estimate=pl.CostEstimate(flops=0, bytes_accessed=2 << 20, transcendentals=0),
        )(slab_sizes, tau_ao)
        return pl.pallas_call(
            functools.partial(kernel, n),
            out_shape=jax.ShapeDtypeStruct((pairs, LANES), f32),
            in_specs=[pl.BlockSpec(memory_space=pl.ANY)] * 3,
            out_specs=pl.BlockSpec(memory_space=pltpu.VMEM),
            scratch_shapes=[
                pltpu.VMEM((slabs, rows, width), bf),
                pltpu.VMEM((width, virtuals), f32),
                pltpu.VMEM((width, virtuals), bf),
                pltpu.VMEM((width, virtuals), bf),
                pltpu.VMEM((slots, virtuals), bf),
                pltpu.VMEM((slots, virtuals), bf),
                pltpu.VMEM((n, pairs, slots), bf),
                pltpu.VMEM((n, 2, 2, pairs, LANES), f32),
                pltpu.VMEM((n, 2, pairs, LANES), f32),
                pltpu.VMEM((n, pairs, LANES), f32),
                pltpu.VMEM((n, pairs, LANES), f32),
                pltpu.VMEM((n, pairs, LANES), f32),
                dma((3,)),
            ] + [dma((n,))] * 8,
            compiler_params=pltpu.CompilerParams(
                collective_id=0, has_side_effects=True, vmem_limit_bytes=56 * 1024 * 1024
            ),
            cost_estimate=pl.CostEstimate(flops=flops, bytes_accessed=4 << 20, transcendentals=0),
        )(amps, integrals, transform)

    return jax.shard_map(
        body,
        mesh=mesh,
        in_specs=(P("pair", None), P(), P("pair", "rep", None), P()),
        out_specs=P("pair", "rep"),
        check_vma=False,
    )
```

time: 147 us -> 40.2 us (0.27)
  waiting for transfers between devices: 86.2 us -> 0 us
  Pallas kernels: 0 us -> 35.9 us
  blocking collectives: 21.6 us -> 0 us
  local copies, waits for them, and re-layouts: 18.7 us -> 4.04 us
  between operations: 13.4 us -> 0.03 us
  matrix products: 5.02 us -> 0 us
  other arithmetic: 2.19 us -> 0 us
    reduce_scatter x2 -> x0, waiting for transfers between devices: 86.2 us -> none  [the longest x1 67.4 us: contract(): lax.psum_scatter(jnp.dot(pair_amps, slab_weights, preferred_element_type=...]
    pallas_call x0 -> x2, Pallas kernels: none -> 35.9 us  [the longest x1 34.2 us: body(): pl.pallas_call(functools.partial(kernel, n), out_shape=jax.ShapeDtypeStru...]
    all_to_all x1 -> x0, blocking collectives: 21.6 us -> none  [regroup(): lax.all_to_all(outgoing, 'pair', split_axis=1, concat_axis=0, tiled=True)]
    gather x2 -> x0, local copies, waits for them, and re-layouts: 14 us -> none  [pick_columns(): picked = jnp.take(tau_rows, columns.reshape(-1), axis=1)]
    dot_general x2 -> x0, matrix products: 5.02 us -> none  [the longest x1 2.96 us: contract(): return jnp.dot(partial_ao, transform, precision=lax.Precision.HIGHEST)]
    unnamed x5 -> x7, local copies, waits for them, and re-layouts: 2.79 us -> 4.04 us
  transfers between devices with their start and end apart: 2 -> 0, of which waited for: 2 -> 0; matrix products, arithmetic and copies ran while one was open for 0% -> 0% of each run, Pallas kernels for 0% -> 0%
where the time goes in v1:
time: 40.2 us; the launch traced here: 40 us
  Pallas kernels  35.9 us (89%)
  local copies, waits for them, and re-layouts  4.04 us (10%)
    pallas_call x1, Pallas kernels, body(): pl.pallas_call(functools.partial(kernel, n), out_shape=jax.ShapeDtypeStru...  34.2 us
    unnamed x7, local copies, waits for them, and re-layouts  4.04 us
    pallas_call x1, Pallas kernels, body(): pl.pallas_call(functools.partial(pick_kernel, n, slabs), out_shape=jax.Sh...  1.77 us

profile of v1, /device:TPU:0, one launch (start us, length us, event | category | flops | bytes accessed | tf_op | source)
XLA Modules:
  0.0 40.0 jit_solution(695296272132737291)
XLA Ops:
  0.0 0.0 copy-start
  0.0 1.2 %copy-done = bf16[64,8192]{1,0:T(8,128)(2,1)S(1)} copy-done((bf16[64,8192]{1,0:T(8,128)(2,1)S(1)}, bf16[64,8192]{1,0:T(8,128)(2,1)}, u32[]{:S(2)}) %copy-start) | copy-done | bytes 1048600
  1.2 0.0 copy-start.2
  1.2 0.7 %copy-done.2 = s32[32]{0:T(128)S(1)} copy-done((s32[32]{0:T(128)S(1)}, s32[32]{0:T(128)}, u32[]{:S(2)}) %copy-start.2) | copy-done | bytes 152
  1.9 1.8 %shard_map.46.amps_out = bf16[8,64,512]{2,1,0:T(8,128)(2,1)S(1)} custom-call(s32[32]{0:T(128)S(1)} %copy-done.2, bf16[64,8192]{1,0:T(8,128)(2,1)S(1)} %copy-done), custom_call_target="tpu_custom_call" | custom-call | bytes 2097152 | tf_op jit(solution)/shard_map/pallas_call | solution.py:192
  3.7 0.0 copy-start.1
  3.7 0.8 %copy-done.1 = bf16[8,64,512]{2,1,0:T(8,128)(2,1)} copy-done((bf16[8,64,512]{2,1,0:T(8,128)(2,1)}, bf16[8,64,512]{2,1,0:T(8,128)(2,1)S(1)}, u32[]{:S(2)}) %copy-start.1) | copy-done | bytes 524312
  4.5 34.2 %shard_map.47 = f32[64,128]{1,0:T(8,128)} custom-call(bf16[8,64,512]{2,1,0:T(8,128)(2,1)} %copy-done.1, bf16[4,128,1024]{2,1,0:T(8,128)(2,1)} %integrals_in.1, f32[1024,512]{1,0:T(8,128)} %transform_in.1), custom_call_target="tpu_custom_call" | custom-call | flops 1610612736 | bytes 4194304 | tf_op jit(solution)/shard_map/pallas_call | solution.py:204
  38.6 1.4 %copy.6 = f32[64,128]{1,0:T(8,128)} copy(f32[64,128]{1,0:T(8,128)} %shard_map.47) | data formatting | bytes 65536
Async XLA Ops:
  0.0 1.2 %copy-start = (bf16[64,8192]{1,0:T(8,128)(2,1)S(1)}, bf16[64,8192]{1,0:T(8,128)(2,1)}, u32[]{:S(2)}) copy-start(bf16[64,8192]{1,0:T(8,128)(2,1)} %tau.1) | copy-start | bytes 3145732
  1.2 0.7 %copy-start.2 = (s32[32]{0:T(128)S(1)}, s32[32]{0:T(128)}, u32[]{:S(2)}) copy-start(s32[32]{0:T(128)} %sizes.1) | copy-start | bytes 388
  3.7 0.8 %copy-start.1 = (bf16[8,64,512]{2,1,0:T(8,128)(2,1)}, bf16[8,64,512]{2,1,0:T(8,128)(2,1)S(1)}, u32[]{:S(2)}) copy-start(bf16[8,64,512]{2,1,0:T(8,128)(2,1)S(1)} %shard_map.46.amps_out) | copy-start | bytes 1572868

commit v2 on v1

--- a/solution.py
+++ b/solution.py
@@ -11,10 +11,12 @@
 LANES = 128
 
 
-def hop(slot, n):
-    u = slot - 1
-    h, odd = lax.div(u + 1, 2), lax.rem(u, 2)
-    return n // 2 + h * (2 * odd - 1)
+def partner(me, slot, n):
+    other, bit = 0, 1
+    while bit < n:
+        other += lax.rem(lax.div(me, bit) + lax.div(slot, bit), 2) * bit
+        bit *= 2
+    return other
 
 
 def pick_kernel(n, slabs, sizes, tau, target, offsets):
@@ -31,13 +33,13 @@
 
     @pl.loop(0, n)
     def _(slot):
-        dest = jnp.where(slot == 0, me, lax.rem(me + hop(slot, n), n))
+        dest = partner(me, slot, n)
         for q in range(slabs):
             slab = dest * slabs + q
             start = jnp.minimum(offsets[slab] + rep * rows, packed - 1)
             base = jnp.minimum(lax.div(start, LANES) * LANES, packed - 2 * LANES)
             window = tau[:, pl.ds(pl.multiple_of(base, LANES), 2 * LANES)].astype(jnp.float32)
-            turned = pltpu.roll(window, 2 * LANES - (start - base), 1)[:, :rows]
+            turned = pltpu.roll(window, lax.rem(2 * LANES - (start - base), 2 * LANES), 1)[:, :rows]
             kept = jnp.where(places < sizes[slab], turned, 0.0)
             target[slot, :, q * rows : (q + 1) * rows] = kept.astype(jnp.bfloat16)
 
@@ -63,14 +65,14 @@
 
     @pl.loop(1, n)
     def _(slot):
-        other = lax.rem(me + hop(slot, n), n)
+        other = partner(me, slot, n)
         pl.semaphore_signal(barrier, inc=1, device_id=(other, rep), device_id_type=MESH)
 
     pl.semaphore_signal(barrier, inc=1, device_id=(me, near), device_id_type=MESH)
     pl.semaphore_signal(barrier, inc=1, device_id=(me, far), device_id_type=MESH)
 
     def send_amps(slot):
-        other = lax.rem(me + hop(slot, n), n)
+        other = partner(me, slot, n)
         return pltpu.make_async_remote_copy(
             src_ref=amps_out.at[slot], dst_ref=amps.at[slot],
             send_sem=amps_send.at[slot], recv_sem=amps_recv.at[slot],
@@ -92,7 +94,7 @@
         )
 
     def send_back(slot):
-        owner = lax.rem(me + n - hop(slot, n), n)
+        owner = partner(me, slot, n)
         return pltpu.make_async_remote_copy(
             src_ref=done.at[slot], dst_ref=back.at[slot],
             send_sem=back_send.at[slot], recv_sem=back_recv.at[slot],
@@ -101,7 +103,11 @@
 
     pl.semaphore_wait(barrier, n + 1)
 
-    @pl.loop(1, n)
+    half = n // 2
+    for slot in (half, half + 1):
+        send_amps(jnp.int32(slot)).start()
+
+    @pl.loop(1, half)
     def _(slot):
         send_amps(slot).start()
 
@@ -132,6 +138,11 @@
         def _():
             send_amps(step).wait_recv()
 
+        @pl.when(jnp.logical_and(step >= half, step < n - 2))
+        def _():
+            send_amps(step).wait_send()
+            send_amps(step + 2).start()
+
         @pl.when(step < n)
         def _():
             block = amps[step]
@@ -171,8 +182,11 @@
     def _(slot):
         @pl.when(slot >= 1)
         def _():
+            send_back(slot).wait_send()
+
+        @pl.when(jnp.logical_or(jnp.logical_and(slot >= 1, slot < half), slot >= n - 2))
+        def _():
             send_amps(slot).wait_send()
-            send_back(slot).wait_send()
 
         send_core(slot).wait_send()
         send_x(slot).wait_send()
@@ -204,7 +218,7 @@
         return pl.pallas_call(
             functools.partial(kernel, n),
             out_shape=jax.ShapeDtypeStruct((pairs, LANES), f32),
-            in_specs=[pl.BlockSpec(memory_space=pl.ANY)] * 3,
+            in_specs=[pl.BlockSpec(memory_space=pl.ANY)] + [pl.BlockSpec(memory_space=pltpu.HBM)] * 2,
             out_specs=pl.BlockSpec(memory_space=pltpu.VMEM),
             scratch_shapes=[
                 pltpu.VMEM((slabs, rows, width), bf),

time: 40.2 us -> 37.9 us (0.943)
  Pallas kernels: 35.9 us -> 33.6 us
    pallas_call x1, Pallas kernels: 34.2 us -> 31.8 us  [body(): pl.pallas_call(functools.partial(kernel, n), out_shape=jax.ShapeDtypeStru...]
where the time goes in v2:
time: 37.9 us; the launch traced here: 37.7 us
  Pallas kernels  33.6 us (89%)
  local copies, waits for them, and re-layouts  4.04 us (11%)
    pallas_call x1, Pallas kernels, body(): pl.pallas_call(functools.partial(kernel, n), out_shape=jax.ShapeDtypeStru...  31.8 us
    unnamed x7, local copies, waits for them, and re-layouts  4.04 us
    pallas_call x1, Pallas kernels, body(): pl.pallas_call(functools.partial(pick_kernel, n, slabs), out_shape=jax.Sh...  1.79 us

profile of v2, /device:TPU:0, one launch (start us, length us, event | category | flops | bytes accessed | tf_op | source)
XLA Modules:
  0.0 37.7 jit_solution(370295387713260367)
XLA Ops:
  0.0 0.0 copy-start
  0.0 1.2 %copy-done = bf16[64,8192]{1,0:T(8,128)(2,1)S(1)} copy-done((bf16[64,8192]{1,0:T(8,128)(2,1)S(1)}, bf16[64,8192]{1,0:T(8,128)(2,1)}, u32[]{:S(2)}) %copy-start) | copy-done | bytes 1048600
  1.2 0.0 copy-start.2
  1.2 0.7 %copy-done.2 = s32[32]{0:T(128)S(1)} copy-done((s32[32]{0:T(128)S(1)}, s32[32]{0:T(128)}, u32[]{:S(2)}) %copy-start.2) | copy-done | bytes 152
  1.9 1.8 %shard_map.46.amps_out = bf16[8,64,512]{2,1,0:T(8,128)(2,1)S(1)} custom-call(s32[32]{0:T(128)S(1)} %copy-done.2, bf16[64,8192]{1,0:T(8,128)(2,1)S(1)} %copy-done), custom_call_target="tpu_custom_call" | custom-call | bytes 2097152 | tf_op jit(solution)/shard_map/pallas_call | solution.py:206
  3.7 0.0 copy-start.1
  3.7 0.8 %copy-done.1 = bf16[8,64,512]{2,1,0:T(8,128)(2,1)} copy-done((bf16[8,64,512]{2,1,0:T(8,128)(2,1)}, bf16[8,64,512]{2,1,0:T(8,128)(2,1)S(1)}, u32[]{:S(2)}) %copy-start.1) | copy-done | bytes 524312
  4.5 31.8 %shard_map.47 = f32[64,128]{1,0:T(8,128)} custom-call(bf16[8,64,512]{2,1,0:T(8,128)(2,1)} %copy-done.1, bf16[4,128,1024]{2,1,0:T(8,128)(2,1)} %integrals_in.1, f32[1024,512]{1,0:T(8,128)} %transform_in.1), custom_call_target="tpu_custom_call" | custom-call | flops 1610612736 | bytes 4194304 | tf_op jit(solution)/shard_map/pallas_call | solution.py:218
  36.3 1.4 %copy.6 = f32[64,128]{1,0:T(8,128)} copy(f32[64,128]{1,0:T(8,128)} %shard_map.47) | data formatting | bytes 65536
Async XLA Ops:
  0.0 1.2 %copy-start = (bf16[64,8192]{1,0:T(8,128)(2,1)S(1)}, bf16[64,8192]{1,0:T(8,128)(2,1)}, u32[]{:S(2)}) copy-start(bf16[64,8192]{1,0:T(8,128)(2,1)} %tau.1) | copy-start | bytes 3145732
  1.2 0.7 %copy-start.2 = (s32[32]{0:T(128)S(1)}, s32[32]{0:T(128)}, u32[]{:S(2)}) copy-start(s32[32]{0:T(128)} %sizes.1) | copy-start | bytes 388
  3.7 0.8 %copy-start.1 = (bf16[8,64,512]{2,1,0:T(8,128)(2,1)}, bf16[8,64,512]{2,1,0:T(8,128)(2,1)S(1)}, u32[]{:S(2)}) copy-start(bf16[8,64,512]{2,1,0:T(8,128)(2,1)S(1)} %shard_map.46.amps_out) | copy-start | bytes 1572868

commit v3 on v2

--- a/solution.py
+++ b/solution.py
@@ -46,8 +46,8 @@
 
 def kernel(
     n, amps_out, integrals_in, transform_in, out,
-    integrals, transform, t_hi, t_lo, w_hi, w_lo, amps, part, core_in, x_in, done, back,
-    load_sem, amps_send, amps_recv, core_send, core_recv, x_send, x_recv, back_send, back_recv,
+    integrals, transform, t_hi, t_lo, w_hi, w_lo, amps, part, core_in, x_in, done, y_in, back,
+    load_sem, amps_send, amps_recv, core_send, core_recv, x_send, x_recv, y_send, y_recv, back_send, back_recv,
 ):
     me, rep = lax.axis_index("pair"), lax.axis_index("rep")
     hi, lo = lax.div(rep, 2), lax.rem(rep, 2)
@@ -93,12 +93,18 @@
             device_id=(me, far), device_id_type=MESH,
         )
 
-    def send_back(slot):
-        owner = partner(me, slot, n)
-        return pltpu.make_async_remote_copy(
-            src_ref=done.at[slot], dst_ref=back.at[slot],
-            send_sem=back_send.at[slot], recv_sem=back_recv.at[slot],
-            device_id=(owner, rep), device_id_type=MESH,
+    def send_y(slot):
+        return pltpu.make_async_remote_copy(
+            src_ref=done.at[slot], dst_ref=y_in.at[slot],
+            send_sem=y_send.at[slot], recv_sem=y_recv.at[slot],
+            device_id=(partner(me, 1, n), rep), device_id_type=MESH,
+        )
+
+    def send_back(duo):
+        return pltpu.make_async_remote_copy(
+            src_ref=done.at[2 * duo], dst_ref=back.at[duo],
+            send_sem=back_send.at[duo], recv_sem=back_recv.at[duo],
+            device_id=(partner(me, 2 * duo, n), rep), device_id_type=MESH,
         )
 
     pl.semaphore_wait(barrier, n + 1)
@@ -132,7 +138,7 @@
 
     load_own.wait()
 
-    @pl.loop(0, n + 2)
+    @pl.loop(0, n + 3)
     def _(step):
         @pl.when(jnp.logical_and(step >= 1, step < n))
         def _():
@@ -161,35 +167,49 @@
             part[slot, lo, 1 - hi] = part[slot, lo, 1 - hi] + core_in[slot, 1 - hi]
             send_x(slot).start()
 
-        @pl.when(step >= 2)
+        @pl.when(jnp.logical_and(step >= 2, step <= n + 1))
         def _():
             slot = step - 2
             send_x(slot).wait_recv()
             done[slot] = part[slot, lo, hi] + core_in[slot, hi] + x_in[slot]
 
-            @pl.when(slot >= 1)
+            @pl.when(lax.rem(slot, 2) == 1)
             def _():
-                send_back(slot).start()
+                send_y(slot).start()
+
+        @pl.when(jnp.logical_and(step >= 4, lax.rem(step, 2) == 0))
+        def _():
+            slot = step - 3
+            send_y(slot).wait_recv()
+            done[slot - 1] = done[slot - 1] + y_in[slot]
+
+            @pl.when(slot >= 3)
+            def _():
+                send_back(lax.div(slot, 2)).start()
 
     out[...] = done[0]
 
-    @pl.loop(1, n)
-    def _(slot):
-        send_back(slot).wait_recv()
-        out[...] = out[...] + back[slot]
+    @pl.loop(1, half)
+    def _(duo):
+        send_back(duo).wait_recv()
+        out[...] = out[...] + back[duo]
 
     @pl.loop(0, n)
     def _(slot):
-        @pl.when(slot >= 1)
-        def _():
-            send_back(slot).wait_send()
-
         @pl.when(jnp.logical_or(jnp.logical_and(slot >= 1, slot < half), slot >= n - 2))
         def _():
             send_amps(slot).wait_send()
+
+        @pl.when(lax.rem(slot, 2) == 1)
+        def _():
+            send_y(slot).wait_send()
 
         send_core(slot).wait_send()
         send_x(slot).wait_send()
+
+    @pl.loop(1, half)
+    def _(duo):
+        send_back(duo).wait_send()
 
 
 def solution(mesh):
@@ -212,13 +232,13 @@
             ],
             out_specs=pl.BlockSpec(memory_space=pltpu.VMEM),
             scratch_shapes=[pltpu.SMEM((slab_sizes.shape[0],), jnp.int32)],
-            compiler_params=pltpu.CompilerParams(vmem_limit_bytes=48 * 1024 * 1024),
+            compiler_params=pltpu.CompilerParams(vmem_limit_bytes=16 << 20),
             cost_estimate=pl.CostEstimate(flops=0, bytes_accessed=2 << 20, transcendentals=0),
         )(slab_sizes, tau_ao)
         return pl.pallas_call(
             functools.partial(kernel, n),
             out_shape=jax.ShapeDtypeStruct((pairs, LANES), f32),
-            in_specs=[pl.BlockSpec(memory_space=pl.ANY)] + [pl.BlockSpec(memory_space=pltpu.HBM)] * 2,
+            in_specs=[pl.BlockSpec(memory_space=pltpu.VMEM)] + [pl.BlockSpec(memory_space=pltpu.HBM)] * 2,
             out_specs=pl.BlockSpec(memory_space=pltpu.VMEM),
             scratch_shapes=[
                 pltpu.VMEM((slabs, rows, width), bf),
@@ -233,10 +253,11 @@
                 pltpu.VMEM((n, pairs, LANES), f32),
                 pltpu.VMEM((n, pairs, LANES), f32),
                 pltpu.VMEM((n, pairs, LANES), f32),
+                pltpu.VMEM((n // 2, pairs, LANES), f32),
                 dma((3,)),
-            ] + [dma((n,))] * 8,
+            ] + [dma((n,))] * 8 + [dma((n // 2,))] * 2,
             compiler_params=pltpu.CompilerParams(
-                collective_id=0, has_side_effects=True, vmem_limit_bytes=56 * 1024 * 1024
+                collective_id=0, has_side_effects=True, vmem_limit_bytes=(14 << 20) + n * (9 << 16)
             ),
             cost_estimate=pl.CostEstimate(flops=flops, bytes_accessed=4 << 20, transcendentals=0),
         )(amps, integrals, transform)

time: 37.9 us -> 40 us (1.055)
  local copies, waits for them, and re-layouts: 4.04 us -> 5.31 us
  Pallas kernels: 33.6 us -> 34.5 us
    unnamed x7 -> x9, local copies, waits for them, and re-layouts: 4.04 us -> 5.31 us
    pallas_call x1, Pallas kernels: 31.8 us -> 32.7 us  [body(): pl.pallas_call(functools.partial(kernel, n), out_shape=jax.ShapeDtypeStru...]
where the time goes in v3:
time: 40 us; the launch traced here: 39.8 us
  Pallas kernels  34.5 us (86%)
  local copies, waits for them, and re-layouts  5.31 us (13%)
    pallas_call x1, Pallas kernels, body(): pl.pallas_call(functools.partial(kernel, n), out_shape=jax.ShapeDtypeStru...  32.7 us
    unnamed x9, local copies, waits for them, and re-layouts  5.31 us
    pallas_call x1, Pallas kernels, body(): pl.pallas_call(functools.partial(pick_kernel, n, slabs), out_shape=jax.Sh...  1.79 us

profile of v3, /device:TPU:0, one launch (start us, length us, event | category | flops | bytes accessed | tf_op | source)
XLA Modules:
  0.0 39.8 jit_solution(6435617178430488153)
XLA Ops:
  0.0 0.0 copy-start
  0.0 1.2 %copy-done = bf16[64,8192]{1,0:T(8,128)(2,1)S(1)} copy-done((bf16[64,8192]{1,0:T(8,128)(2,1)S(1)}, bf16[64,8192]{1,0:T(8,128)(2,1)}, u32[]{:S(2)}) %copy-start) | copy-done | bytes 1048600
  1.2 0.0 copy-start.1
  1.2 0.7 %copy-done.1 = s32[32]{0:T(128)S(1)} copy-done((s32[32]{0:T(128)S(1)}, s32[32]{0:T(128)}, u32[]{:S(2)}) %copy-start.1) | copy-done | bytes 152
  1.9 1.8 %shard_map.46.amps_out = bf16[8,64,512]{2,1,0:T(8,128)(2,1)S(1)} custom-call(s32[32]{0:T(128)S(1)} %copy-done.1, bf16[64,8192]{1,0:T(8,128)(2,1)S(1)} %copy-done), custom_call_target="tpu_custom_call" | custom-call | bytes 2097152 | tf_op jit(solution)/shard_map/pallas_call | solution.py:226
  3.7 0.0 copy-start.2
  3.7 1.6 %copy-done.2 = f32[1024,512]{1,0:T(8,128)S(1)} copy-done((f32[1024,512]{1,0:T(8,128)S(1)}, f32[1024,512]{1,0:T(8,128)}, u32[]{:S(2)}) %copy-start.2) | copy-done | bytes 2097176
  5.3 0.0 copy-start.3
  5.3 1.2 %copy-done.3 = bf16[4,128,1024]{2,1,0:T(8,128)(2,1)S(1)} copy-done((bf16[4,128,1024]{2,1,0:T(8,128)(2,1)S(1)}, bf16[4,128,1024]{2,1,0:T(8,128)(2,1)}, u32[]{:S(2)}) %copy-start.3) | copy-done | bytes 1048600
  6.5 32.7 %shard_map.47 = f32[64,128]{1,0:T(8,128)S(1)} custom-call(bf16[8,64,512]{2,1,0:T(8,128)(2,1)S(1)} %shard_map.46.amps_out, bf16[4,128,1024]{2,1,0:T(8,128)(2,1)S(1)} %copy-done.3, f32[1024,512]{1,0:T(8,128)S(1)} %copy-done.2), custom_call_target="tpu_custom_call" | custom-call | flops 1610612736 | bytes 4194304 | tf_op jit(solution)/shard_map/pallas_call | solution.py:238
  39.2 0.6 %copy.6 = f32[64,128]{1,0:T(8,128)} copy(f32[64,128]{1,0:T(8,128)S(1)} %shard_map.47) | data formatting | bytes 65536
Async XLA Ops:
  0.0 1.2 %copy-start = (bf16[64,8192]{1,0:T(8,128)(2,1)S(1)}, bf16[64,8192]{1,0:T(8,128)(2,1)}, u32[]{:S(2)}) copy-start(bf16[64,8192]{1,0:T(8,128)(2,1)} %tau.1) | copy-start | bytes 3145732
  1.2 0.7 %copy-start.1 = (s32[32]{0:T(128)S(1)}, s32[32]{0:T(128)}, u32[]{:S(2)}) copy-start(s32[32]{0:T(128)} %sizes.1) | copy-start | bytes 388
  3.7 1.6 %copy-start.2 = (f32[1024,512]{1,0:T(8,128)S(1)}, f32[1024,512]{1,0:T(8,128)}, u32[]{:S(2)}) copy-start(f32[1024,512]{1,0:T(8,128)} %transform_in.1) | copy-start | bytes 6291460
  5.3 1.2 %copy-start.3 = (bf16[4,128,1024]{2,1,0:T(8,128)(2,1)S(1)}, bf16[4,128,1024]{2,1,0:T(8,128)(2,1)}, u32[]{:S(2)}) copy-start(bf16[4,128,1024]{2,1,0:T(8,128)(2,1)} %integrals_in.1) | copy-start | bytes 3145732

commit v4 on v2

--- a/solution.py
+++ b/solution.py
@@ -132,44 +132,51 @@
 
     load_own.wait()
 
-    @pl.loop(0, n + 2)
-    def _(step):
-        @pl.when(jnp.logical_and(step >= 1, step < n))
-        def _():
-            send_amps(step).wait_recv()
-
-        @pl.when(jnp.logical_and(step >= half, step < n - 2))
-        def _():
-            send_amps(step).wait_send()
-            send_amps(step + 2).start()
-
-        @pl.when(step < n)
-        def _():
-            block = amps[step]
+    def multiply(first, last):
+        @pl.loop(first, last)
+        def _(slot):
+            @pl.when(slot >= 1)
+            def _():
+                send_amps(slot).wait_recv()
+
+            @pl.when(jnp.logical_and(slot >= half, slot < n - 2))
+            def _():
+                send_amps(slot).wait_send()
+                send_amps(slot + 2).start()
+
+            block = amps[slot]
             for h in range(2):
                 columns = slice(h * 2 * LANES, (h + 1) * 2 * LANES)
                 p = jnp.dot(block, w_lo[:, columns], preferred_element_type=jnp.float32)
                 p += jnp.dot(block, w_hi[:, columns], preferred_element_type=jnp.float32)
-                part[step, 0, h] = p[:, :LANES]
-                part[step, 1, h] = p[:, LANES:]
-            send_core(step).start()
-
-        @pl.when(jnp.logical_and(step >= 1, step <= n))
-        def _():
-            slot = step - 1
+                part[slot, 0, h] = p[:, :LANES]
+                part[slot, 1, h] = p[:, LANES:]
+            send_core(slot).start()
+
+    def sum_core(first, last):
+        @pl.loop(first, last)
+        def _(slot):
             send_core(slot).wait_recv()
             part[slot, lo, 1 - hi] = part[slot, lo, 1 - hi] + core_in[slot, 1 - hi]
             send_x(slot).start()
 
-        @pl.when(step >= 2)
-        def _():
-            slot = step - 2
+    def sum_x(first, last):
+        @pl.loop(first, last)
+        def _(slot):
             send_x(slot).wait_recv()
             done[slot] = part[slot, lo, hi] + core_in[slot, hi] + x_in[slot]
 
             @pl.when(slot >= 1)
             def _():
                 send_back(slot).start()
+
+    groups = [(0, half)] + [(at, at + 2) for at in range(half, n, 2)]
+    for at, group in enumerate(groups):
+        multiply(*group)
+        if at:
+            sum_x(*groups[at - 1])
+        sum_core(*group)
+    sum_x(*groups[-1])
 
     out[...] = done[0]
 
@@ -218,7 +225,7 @@
         return pl.pallas_call(
             functools.partial(kernel, n),
             out_shape=jax.ShapeDtypeStruct((pairs, LANES), f32),
-            in_specs=[pl.BlockSpec(memory_space=pl.ANY)] + [pl.BlockSpec(memory_space=pltpu.HBM)] * 2,
+            in_specs=[pl.BlockSpec(memory_space=pltpu.VMEM)] + [pl.BlockSpec(memory_space=pltpu.HBM)] * 2,
             out_specs=pl.BlockSpec(memory_space=pltpu.VMEM),
             scratch_shapes=[
                 pltpu.VMEM((slabs, rows, width), bf),
@@ -236,7 +243,7 @@
                 dma((3,)),
             ] + [dma((n,))] * 8,
             compiler_params=pltpu.CompilerParams(
-                collective_id=0, has_side_effects=True, vmem_limit_bytes=56 * 1024 * 1024
+                collective_id=0, has_side_effects=True, vmem_limit_bytes=211 << 18
             ),
             cost_estimate=pl.CostEstimate(flops=flops, bytes_accessed=4 << 20, transcendentals=0),
         )(amps, integrals, transform)

time: 37.9 us -> 33.7 us (0.89)
  Pallas kernels: 33.6 us -> 31.1 us
  local copies, waits for them, and re-layouts: 4.04 us -> 2.5 us
    pallas_call x1, Pallas kernels: 31.8 us -> 29.3 us  [body(): pl.pallas_call(functools.partial(kernel, n), out_shape=jax.ShapeDtypeStru...]
    unnamed x7 -> x5, local copies, waits for them, and re-layouts: 4.04 us -> 2.5 us
where the time goes in v4:
time: 33.7 us; the launch traced here: 33.6 us
  Pallas kernels  31.1 us (92%)
  local copies, waits for them, and re-layouts  2.5 us (7%)
    pallas_call x1, Pallas kernels, body(): pl.pallas_call(functools.partial(kernel, n), out_shape=jax.ShapeDtypeStru...  29.3 us
    unnamed x5, local copies, waits for them, and re-layouts  2.5 us
    pallas_call x1, Pallas kernels, body(): pl.pallas_call(functools.partial(pick_kernel, n, slabs), out_shape=jax.Sh...  1.79 us

profile of v4, /device:TPU:0, one launch (start us, length us, event | category | flops | bytes accessed | tf_op | source)
XLA Modules:
  0.0 33.6 jit_solution(16226268791113030581)
XLA Ops:
  0.0 0.0 copy-start
  0.0 1.2 %copy-done = bf16[64,8192]{1,0:T(8,128)(2,1)S(1)} copy-done((bf16[64,8192]{1,0:T(8,128)(2,1)S(1)}, bf16[64,8192]{1,0:T(8,128)(2,1)}, u32[]{:S(2)}) %copy-start) | copy-done | bytes 1048600
  1.2 0.0 copy-start.1
  1.2 0.7 %copy-done.1 = s32[32]{0:T(128)S(1)} copy-done((s32[32]{0:T(128)S(1)}, s32[32]{0:T(128)}, u32[]{:S(2)}) %copy-start.1) | copy-done | bytes 152
  1.9 1.8 %shard_map.46.amps_out = bf16[8,64,512]{2,1,0:T(8,128)(2,1)S(1)} custom-call(s32[32]{0:T(128)S(1)} %copy-done.1, bf16[64,8192]{1,0:T(8,128)(2,1)S(1)} %copy-done), custom_call_target="tpu_custom_call" | custom-call | bytes 2097152 | tf_op jit(solution)/shard_map/pallas_call | solution.py:213
  3.7 29.3 %shard_map.47 = f32[64,128]{1,0:T(8,128)S(1)} custom-call(bf16[8,64,512]{2,1,0:T(8,128)(2,1)S(1)} %shard_map.46.amps_out, bf16[4,128,1024]{2,1,0:T(8,128)(2,1)} %integrals_in.1, f32[1024,512]{1,0:T(8,128)} %transform_in.1), custom_call_target="tpu_custom_call" | custom-call | flops 1610612736 | bytes 4194304 | tf_op jit(solution)/shard_map/pallas_call | solution.py:225
  33.0 0.6 %copy.6 = f32[64,128]{1,0:T(8,128)} copy(f32[64,128]{1,0:T(8,128)S(1)} %shard_map.47) | data formatting | bytes 65536
Async XLA Ops:
  0.0 1.2 %copy-start = (bf16[64,8192]{1,0:T(8,128)(2,1)S(1)}, bf16[64,8192]{1,0:T(8,128)(2,1)}, u32[]{:S(2)}) copy-start(bf16[64,8192]{1,0:T(8,128)(2,1)} %tau.1) | copy-start | bytes 3145732
  1.2 0.7 %copy-start.1 = (s32[32]{0:T(128)S(1)}, s32[32]{0:T(128)}, u32[]{:S(2)}) copy-start(s32[32]{0:T(128)} %sizes.1) | copy-start | bytes 388

commit v5 on v4

--- a/solution.py
+++ b/solution.py
@@ -19,17 +19,24 @@
     return other
 
 
-def pick_kernel(n, slabs, sizes, tau, target, offsets):
+def pick_kernel(n, slabs, sizes_in, tau_in, target, offsets, sizes, tau, load_sem):
     me, rep = lax.axis_index("pair"), lax.axis_index("rep")
     pairs, packed = tau.shape
     rows = target.shape[2] // slabs
 
+    load_sizes = pltpu.make_async_copy(sizes_in, sizes, load_sem.at[0])
+    load_tau = pltpu.make_async_copy(tau_in, tau, load_sem.at[1])
+    load_sizes.start()
+    load_tau.start()
+    load_sizes.wait()
+
     def add_up(s, total):
         offsets[s] = total
         return total + sizes[s]
 
     lax.fori_loop(0, sizes.shape[0], add_up, jnp.int32(0))
     places = lax.broadcasted_iota(jnp.int32, (pairs, rows), 1) + rep * rows
+    load_tau.wait()
 
     @pl.loop(0, n)
     def _(slot):
@@ -104,8 +111,10 @@
     pl.semaphore_wait(barrier, n + 1)
 
     half = n // 2
-    for slot in (half, half + 1):
-        send_amps(jnp.int32(slot)).start()
+
+    @pl.loop(half, n)
+    def _(slot):
+        send_amps(slot).start()
 
     @pl.loop(1, half)
     def _(slot):
@@ -139,11 +148,6 @@
             def _():
                 send_amps(slot).wait_recv()
 
-            @pl.when(jnp.logical_and(slot >= half, slot < n - 2))
-            def _():
-                send_amps(slot).wait_send()
-                send_amps(slot + 2).start()
-
             block = amps[slot]
             for h in range(2):
                 columns = slice(h * 2 * LANES, (h + 1) * 2 * LANES)
@@ -189,11 +193,8 @@
     def _(slot):
         @pl.when(slot >= 1)
         def _():
+            send_amps(slot).wait_send()
             send_back(slot).wait_send()
-
-        @pl.when(jnp.logical_or(jnp.logical_and(slot >= 1, slot < half), slot >= n - 2))
-        def _():
-            send_amps(slot).wait_send()
 
         send_core(slot).wait_send()
         send_x(slot).wait_send()
@@ -213,13 +214,13 @@
         amps = pl.pallas_call(
             functools.partial(pick_kernel, n, slabs),
             out_shape=jax.ShapeDtypeStruct((n, pairs, slots), bf),
-            in_specs=[
-                pl.BlockSpec(memory_space=pltpu.SMEM),
-                pl.BlockSpec(memory_space=pltpu.VMEM),
+            in_specs=[pl.BlockSpec(memory_space=pltpu.HBM)] * 2,
+            out_specs=pl.BlockSpec(memory_space=pltpu.VMEM),
+            scratch_shapes=[pltpu.SMEM((slab_sizes.shape[0],), jnp.int32)] * 2 + [
+                pltpu.VMEM((pairs, packed), bf),
+                dma((2,)),
             ],
-            out_specs=pl.BlockSpec(memory_space=pltpu.VMEM),
-            scratch_shapes=[pltpu.SMEM((slab_sizes.shape[0],), jnp.int32)],
-            compiler_params=pltpu.CompilerParams(vmem_limit_bytes=48 * 1024 * 1024),
+            compiler_params=pltpu.CompilerParams(vmem_limit_bytes=211 << 18),
             cost_estimate=pl.CostEstimate(flops=0, bytes_accessed=2 << 20, transcendentals=0),
         )(slab_sizes, tau_ao)
         return pl.pallas_call(

time: 33.7 us -> 33.5 us (level)
  local copies, waits for them, and re-layouts: 2.5 us -> 1.27 us
  Pallas kernels: 31.1 us -> 32.1 us
    unnamed x5 -> x3, local copies, waits for them, and re-layouts: 2.5 us -> 1.27 us
    pallas_call x1, Pallas kernels: 29.3 us -> 29.8 us  [body(): pl.pallas_call(functools.partial(kernel, n), out_shape=jax.ShapeDtypeStru...]
    pallas_call x1, Pallas kernels: 1.79 us -> 2.26 us  [body(): pl.pallas_call(functools.partial(pick_kernel, n, slabs), out_shape=jax.Sh...]
where the time goes in v5:
time: 33.5 us; the launch traced here: 33.4 us
  Pallas kernels  32.1 us (96%)
  local copies, waits for them, and re-layouts  1.27 us (4%)
    pallas_call x1, Pallas kernels, body(): pl.pallas_call(functools.partial(kernel, n), out_shape=jax.ShapeDtypeStru...  29.8 us
    pallas_call x1, Pallas kernels, body(): pl.pallas_call(functools.partial(pick_kernel, n, slabs), out_shape=jax.Sh...  2.26 us
    unnamed x3, local copies, waits for them, and re-layouts  1.27 us

profile of v5, /device:TPU:0, one launch (start us, length us, event | category | flops | bytes accessed | tf_op | source)
XLA Modules:
  0.0 33.4 jit_solution(2572944358688495711)
XLA Ops:
  0.0 0.0 copy-start
  0.0 0.7 %copy-done = s32[32]{0:T(128)S(1)} copy-done((s32[32]{0:T(128)S(1)}, s32[32]{0:T(128)}, u32[]{:S(2)}) %copy-start) | copy-done | bytes 152
  0.7 2.3 %shard_map.46.amps_out = bf16[8,64,512]{2,1,0:T(8,128)(2,1)S(1)} custom-call(s32[32]{0:T(128)S(1)} %copy-done, bf16[64,8192]{1,0:T(8,128)(2,1)} %tau_in.1), custom_call_target="tpu_custom_call" | custom-call | bytes 2097152 | tf_op jit(solution)/shard_map/pallas_call | solution.py:214
  2.9 29.8 %shard_map.47 = f32[64,128]{1,0:T(8,128)S(1)} custom-call(bf16[8,64,512]{2,1,0:T(8,128)(2,1)S(1)} %shard_map.46.amps_out, bf16[4,128,1024]{2,1,0:T(8,128)(2,1)} %integrals_in.1, f32[1024,512]{1,0:T(8,128)} %transform_in.1), custom_call_target="tpu_custom_call" | custom-call | flops 1610612736 | bytes 4194304 | tf_op jit(solution)/shard_map/pallas_call | solution.py:226
  32.8 0.6 %copy.6 = f32[64,128]{1,0:T(8,128)} copy(f32[64,128]{1,0:T(8,128)S(1)} %shard_map.47) | data formatting | bytes 65536
Async XLA Ops:
  0.0 0.7 %copy-start = (s32[32]{0:T(128)S(1)}, s32[32]{0:T(128)}, u32[]{:S(2)}) copy-start(s32[32]{0:T(128)} %sizes_in.1) | copy-start | bytes 388

commit v6 on v5

--- a/solution.py
+++ b/solution.py
@@ -9,6 +9,7 @@
 
 MESH = pl.DeviceIdType.MESH
 LANES = 128
+AHEAD = 3
 
 
 def partner(me, slot, n):
@@ -112,7 +113,7 @@
 
     half = n // 2
 
-    @pl.loop(half, n)
+    @pl.loop(half, half + AHEAD)
     def _(slot):
         send_amps(slot).start()
 
@@ -148,6 +149,11 @@
             def _():
                 send_amps(slot).wait_recv()
 
+            @pl.when(jnp.logical_and(slot >= half, slot < n - AHEAD))
+            def _():
+                send_amps(slot).wait_send()
+                send_amps(slot + AHEAD).start()
+
             block = amps[slot]
             for h in range(2):
                 columns = slice(h * 2 * LANES, (h + 1) * 2 * LANES)
@@ -174,7 +180,7 @@
             def _():
                 send_back(slot).start()
 
-    groups = [(0, half)] + [(at, at + 2) for at in range(half, n, 2)]
+    groups = [(0, half)] + [(at, min(at + AHEAD, n)) for at in range(half, n, AHEAD)]
     for at, group in enumerate(groups):
         multiply(*group)
         if at:
@@ -193,8 +199,11 @@
     def _(slot):
         @pl.when(slot >= 1)
         def _():
+            send_back(slot).wait_send()
+
+        @pl.when(jnp.logical_or(jnp.logical_and(slot >= 1, slot < half), slot >= n - AHEAD))
+        def _():
             send_amps(slot).wait_send()
-            send_back(slot).wait_send()
 
         send_core(slot).wait_send()
         send_x(slot).wait_send()

time: 33.5 us -> 32.5 us (0.970)
  Pallas kernels: 32.1 us -> 31 us
    pallas_call x1, Pallas kernels: 29.8 us -> 28.8 us  [body(): pl.pallas_call(functools.partial(kernel, n), out_shape=jax.ShapeDtypeStru...]
where the time goes in v6:
time: 32.5 us; the launch traced here: 32.3 us
  Pallas kernels  31 us (95%)
  local copies, waits for them, and re-layouts  1.27 us (4%)
    pallas_call x1, Pallas kernels, body(): pl.pallas_call(functools.partial(kernel, n), out_shape=jax.ShapeDtypeStru...  28.8 us
    pallas_call x1, Pallas kernels, body(): pl.pallas_call(functools.partial(pick_kernel, n, slabs), out_shape=jax.Sh...  2.26 us
    unnamed x3, local copies, waits for them, and re-layouts  1.27 us

profile of v6, /device:TPU:0, one launch (start us, length us, event | category | flops | bytes accessed | tf_op | source)
XLA Modules:
  0.0 32.3 jit_solution(11297784276522646358)
XLA Ops:
  0.0 0.0 copy-start
  0.0 0.7 %copy-done = s32[32]{0:T(128)S(1)} copy-done((s32[32]{0:T(128)S(1)}, s32[32]{0:T(128)}, u32[]{:S(2)}) %copy-start) | copy-done | bytes 152
  0.7 2.3 %shard_map.46.amps_out = bf16[8,64,512]{2,1,0:T(8,128)(2,1)S(1)} custom-call(s32[32]{0:T(128)S(1)} %copy-done, bf16[64,8192]{1,0:T(8,128)(2,1)} %tau_in.1), custom_call_target="tpu_custom_call" | custom-call | bytes 2097152 | tf_op jit(solution)/shard_map/pallas_call | solution.py:223
  2.9 28.8 %shard_map.47 = f32[64,128]{1,0:T(8,128)S(1)} custom-call(bf16[8,64,512]{2,1,0:T(8,128)(2,1)S(1)} %shard_map.46.amps_out, bf16[4,128,1024]{2,1,0:T(8,128)(2,1)} %integrals_in.1, f32[1024,512]{1,0:T(8,128)} %transform_in.1), custom_call_target="tpu_custom_call" | custom-call | flops 1610612736 | bytes 4194304 | tf_op jit(solution)/shard_map/pallas_call | solution.py:235
  31.7 0.6 %copy.6 = f32[64,128]{1,0:T(8,128)} copy(f32[64,128]{1,0:T(8,128)S(1)} %shard_map.47) | data formatting | bytes 65536
Async XLA Ops:
  0.0 0.7 %copy-start = (s32[32]{0:T(128)S(1)}, s32[32]{0:T(128)}, u32[]{:S(2)}) copy-start(s32[32]{0:T(128)} %sizes_in.1) | copy-start | bytes 388

commit v7 on v6

--- a/solution.py
+++ b/solution.py
@@ -54,8 +54,8 @@
 
 def kernel(
     n, amps_out, integrals_in, transform_in, out,
-    integrals, transform, t_hi, t_lo, w_hi, w_lo, amps, part, core_in, x_in, done, back,
-    load_sem, amps_send, amps_recv, core_send, core_recv, x_send, x_recv, back_send, back_recv,
+    integrals, transform, t_hi, t_lo, w_hi, w_lo, amps, part, core_in, x_in, done, y_in, back,
+    load_sem, amps_send, amps_recv, core_send, core_recv, x_send, x_recv, y_send, y_recv, back_send, back_recv,
 ):
     me, rep = lax.axis_index("pair"), lax.axis_index("rep")
     hi, lo = lax.div(rep, 2), lax.rem(rep, 2)
@@ -101,12 +101,18 @@
             device_id=(me, far), device_id_type=MESH,
         )
 
-    def send_back(slot):
-        owner = partner(me, slot, n)
-        return pltpu.make_async_remote_copy(
-            src_ref=done.at[slot], dst_ref=back.at[slot],
-            send_sem=back_send.at[slot], recv_sem=back_recv.at[slot],
-            device_id=(owner, rep), device_id_type=MESH,
+    def send_y(slot):
+        return pltpu.make_async_remote_copy(
+            src_ref=done.at[slot], dst_ref=y_in.at[slot],
+            send_sem=y_send.at[slot], recv_sem=y_recv.at[slot],
+            device_id=(partner(me, 1, n), rep), device_id_type=MESH,
+        )
+
+    def send_back(duo):
+        return pltpu.make_async_remote_copy(
+            src_ref=done.at[2 * duo], dst_ref=back.at[duo],
+            send_sem=back_send.at[duo], recv_sem=back_recv.at[duo],
+            device_id=(partner(me, 2 * duo, n), rep), device_id_type=MESH,
         )
 
     pl.semaphore_wait(barrier, n + 1)
@@ -176,9 +182,19 @@
             send_x(slot).wait_recv()
             done[slot] = part[slot, lo, hi] + core_in[slot, hi] + x_in[slot]
 
-            @pl.when(slot >= 1)
-            def _():
-                send_back(slot).start()
+            @pl.when(lax.rem(slot, 2) == 1)
+            def _():
+                send_y(slot).start()
+
+    def sum_y(first, last):
+        @pl.loop(first // 2, last // 2)
+        def _(duo):
+            send_y(2 * duo + 1).wait_recv()
+            done[2 * duo] = done[2 * duo] + y_in[2 * duo + 1]
+
+            @pl.when(duo >= 1)
+            def _():
+                send_back(duo).start()
 
     groups = [(0, half)] + [(at, min(at + AHEAD, n)) for at in range(half, n, AHEAD)]
     for at, group in enumerate(groups):
@@ -186,27 +202,34 @@
         if at:
             sum_x(*groups[at - 1])
         sum_core(*group)
+        if at:
+            sum_y(*groups[at - 1])
     sum_x(*groups[-1])
+    sum_y(*groups[-1])
 
     out[...] = done[0]
 
-    @pl.loop(1, n)
-    def _(slot):
-        send_back(slot).wait_recv()
-        out[...] = out[...] + back[slot]
+    @pl.loop(1, half)
+    def _(duo):
+        send_back(duo).wait_recv()
+        out[...] = out[...] + back[duo]
 
     @pl.loop(0, n)
     def _(slot):
-        @pl.when(slot >= 1)
-        def _():
-            send_back(slot).wait_send()
-
         @pl.when(jnp.logical_or(jnp.logical_and(slot >= 1, slot < half), slot >= n - AHEAD))
         def _():
             send_amps(slot).wait_send()
 
+        @pl.when(lax.rem(slot, 2) == 1)
+        def _():
+            send_y(slot).wait_send()
+
         send_core(slot).wait_send()
         send_x(slot).wait_send()
+
+    @pl.loop(1, half)
+    def _(duo):
+        send_back(duo).wait_send()
 
 
 def solution(mesh):
@@ -250,8 +273,9 @@
                 pltpu.VMEM((n, pairs, LANES), f32),
                 pltpu.VMEM((n, pairs, LANES), f32),
                 pltpu.VMEM((n, pairs, LANES), f32),
+                pltpu.VMEM((n // 2, pairs, LANES), f32),
                 dma((3,)),
-            ] + [dma((n,))] * 8,
+            ] + [dma((n,))] * 8 + [dma((n // 2,))] * 2,
             compiler_params=pltpu.CompilerParams(
                 collective_id=0, has_side_effects=True, vmem_limit_bytes=211 << 18
             ),

time: 32.5 us -> 35 us (1.077)
  Pallas kernels: 31 us -> 33.6 us
    pallas_call x1, Pallas kernels: 28.8 us -> 31.3 us  [body(): pl.pallas_call(functools.partial(kernel, n), out_shape=jax.ShapeDtypeStru...]
where the time goes in v7:
time: 35 us; the launch traced here: 34.9 us
  Pallas kernels  33.6 us (96%)
  local copies, waits for them, and re-layouts  1.27 us (4%)
    pallas_call x1, Pallas kernels, body(): pl.pallas_call(functools.partial(kernel, n), out_shape=jax.ShapeDtypeStru...  31.3 us
    pallas_call x1, Pallas kernels, body(): pl.pallas_call(functools.partial(pick_kernel, n, slabs), out_shape=jax.Sh...  2.26 us
    unnamed x3, local copies, waits for them, and re-layouts  1.27 us

profile of v7, /device:TPU:0, one launch (start us, length us, event | category | flops | bytes accessed | tf_op | source)
XLA Modules:
  0.0 34.9 jit_solution(6131751680735558424)
XLA Ops:
  0.0 0.0 copy-start
  0.0 0.7 %copy-done = s32[32]{0:T(128)S(1)} copy-done((s32[32]{0:T(128)S(1)}, s32[32]{0:T(128)}, u32[]{:S(2)}) %copy-start) | copy-done | bytes 152
  0.7 2.3 %shard_map.46.amps_out = bf16[8,64,512]{2,1,0:T(8,128)(2,1)S(1)} custom-call(s32[32]{0:T(128)S(1)} %copy-done, bf16[64,8192]{1,0:T(8,128)(2,1)} %tau_in.1), custom_call_target="tpu_custom_call" | custom-call | bytes 2097152 | tf_op jit(solution)/shard_map/pallas_call | solution.py:246
  2.9 31.3 %shard_map.47 = f32[64,128]{1,0:T(8,128)S(1)} custom-call(bf16[8,64,512]{2,1,0:T(8,128)(2,1)S(1)} %shard_map.46.amps_out, bf16[4,128,1024]{2,1,0:T(8,128)(2,1)} %integrals_in.1, f32[1024,512]{1,0:T(8,128)} %transform_in.1), custom_call_target="tpu_custom_call" | custom-call | flops 1610612736 | bytes 4194304 | tf_op jit(solution)/shard_map/pallas_call | solution.py:258
  34.3 0.6 %copy.6 = f32[64,128]{1,0:T(8,128)} copy(f32[64,128]{1,0:T(8,128)S(1)} %shard_map.47) | data formatting | bytes 65536
Async XLA Ops:
  0.0 0.7 %copy-start = (s32[32]{0:T(128)S(1)}, s32[32]{0:T(128)}, u32[]{:S(2)}) copy-start(s32[32]{0:T(128)} %sizes_in.1) | copy-start | bytes 388

commit v8 on v6

--- a/solution.py
+++ b/solution.py
@@ -53,13 +53,11 @@
 
 
 def kernel(
-    n, amps_out, integrals_in, transform_in, out,
-    integrals, transform, t_hi, t_lo, w_hi, w_lo, amps, part, core_in, x_in, done, back,
-    load_sem, amps_send, amps_recv, core_send, core_recv, x_send, x_recv, back_send, back_recv,
+    n, reps, groups, amps_out, integrals_in, transform_in, out,
+    integrals, transform, t_hi, t_lo, w_hi, w_lo, amps, part, rep_in, done, back,
+    load_sem, amps_send, amps_recv, rep_send, rep_recv, back_send, back_recv,
 ):
     me, rep = lax.axis_index("pair"), lax.axis_index("rep")
-    hi, lo = lax.div(rep, 2), lax.rem(rep, 2)
-    near, far = hi * 2 + (1 - lo), (1 - hi) * 2 + lo
     slabs, rows, width = integrals.shape
 
     load_own = pltpu.make_async_copy(amps_out.at[0], amps.at[0], load_sem.at[0])
@@ -76,8 +74,8 @@
         other = partner(me, slot, n)
         pl.semaphore_signal(barrier, inc=1, device_id=(other, rep), device_id_type=MESH)
 
-    pl.semaphore_signal(barrier, inc=1, device_id=(me, near), device_id_type=MESH)
-    pl.semaphore_signal(barrier, inc=1, device_id=(me, far), device_id_type=MESH)
+    for d in range(1, reps):
+        pl.semaphore_signal(barrier, inc=1, device_id=(me, partner(rep, d, reps)), device_id_type=MESH)
 
     def send_amps(slot):
         other = partner(me, slot, n)
@@ -87,18 +85,14 @@
             device_id=(other, rep), device_id_type=MESH,
         )
 
-    def send_core(slot):
+    def send_rep(d, at):
+        first, last = groups[at]
+        held = pl.ds(first, last - first)
+        other = partner(rep, d, reps)
         return pltpu.make_async_remote_copy(
-            src_ref=part.at[slot, 1 - lo], dst_ref=core_in.at[slot],
-            send_sem=core_send.at[slot], recv_sem=core_recv.at[slot],
-            device_id=(me, near), device_id_type=MESH,
-        )
-
-    def send_x(slot):
-        return pltpu.make_async_remote_copy(
-            src_ref=part.at[slot, lo, 1 - hi], dst_ref=x_in.at[slot],
-            send_sem=x_send.at[slot], recv_sem=x_recv.at[slot],
-            device_id=(me, far), device_id_type=MESH,
+            src_ref=part.at[other, held], dst_ref=rep_in.at[d - 1, held],
+            send_sem=rep_send.at[d - 1, at], recv_sem=rep_recv.at[d - 1, at],
+            device_id=(me, other), device_id_type=MESH,
         )
 
     def send_back(slot):
@@ -109,7 +103,7 @@
             device_id=(owner, rep), device_id_type=MESH,
         )
 
-    pl.semaphore_wait(barrier, n + 1)
+    pl.semaphore_wait(barrier, n + reps - 2)
 
     half = n // 2
 
@@ -159,34 +153,30 @@
                 columns = slice(h * 2 * LANES, (h + 1) * 2 * LANES)
                 p = jnp.dot(block, w_lo[:, columns], preferred_element_type=jnp.float32)
                 p += jnp.dot(block, w_hi[:, columns], preferred_element_type=jnp.float32)
-                part[slot, 0, h] = p[:, :LANES]
-                part[slot, 1, h] = p[:, LANES:]
-            send_core(slot).start()
-
-    def sum_core(first, last):
+                part[2 * h, slot] = p[:, :LANES]
+                part[2 * h + 1, slot] = p[:, LANES:]
+
+    def sum_rep(first, last):
         @pl.loop(first, last)
         def _(slot):
-            send_core(slot).wait_recv()
-            part[slot, lo, 1 - hi] = part[slot, lo, 1 - hi] + core_in[slot, 1 - hi]
-            send_x(slot).start()
-
-    def sum_x(first, last):
-        @pl.loop(first, last)
-        def _(slot):
-            send_x(slot).wait_recv()
-            done[slot] = part[slot, lo, hi] + core_in[slot, hi] + x_in[slot]
+            total = part[rep, slot]
+            for d in range(1, reps):
+                total = total + rep_in[d - 1, slot]
+            done[slot] = total
 
             @pl.when(slot >= 1)
             def _():
                 send_back(slot).start()
 
-    groups = [(0, half)] + [(at, min(at + AHEAD, n)) for at in range(half, n, AHEAD)]
-    for at, group in enumerate(groups):
-        multiply(*group)
+    for at in range(len(groups) + 1):
+        if at < len(groups):
+            multiply(*groups[at])
+            for d in range(1, reps):
+                send_rep(d, at).start()
         if at:
-            sum_x(*groups[at - 1])
-        sum_core(*group)
-    sum_x(*groups[-1])
+            for d in range(1, reps):
+                send_rep(d, at - 1).wait_recv()
+            sum_rep(*groups[at - 1])
 
     out[...] = done[0]
 
@@ -205,8 +195,9 @@
         def _():
             send_amps(slot).wait_send()
 
-        send_core(slot).wait_send()
-        send_x(slot).wait_send()
+    for at in range(len(groups)):
+        for d in range(1, reps):
+            send_rep(d, at).wait_send()
 
 
 def solution(mesh):
@@ -218,6 +209,8 @@
         virtuals = transform.shape[1]
         assert reps == 4 and rows == LANES and virtuals == reps * LANES
         slots = slabs * rows
+        half = n // 2
+        groups = [(0, half)] + [(at, min(at + AHEAD, n)) for at in range(half, n, AHEAD)]
         bf, f32, dma = jnp.bfloat16, jnp.float32, pltpu.SemaphoreType.DMA
         flops = 4 * slots * width * virtuals + 4 * n * pairs * slots * virtuals
         amps = pl.pallas_call(
@@ -233,7 +226,7 @@
             cost_estimate=pl.CostEstimate(flops=0, bytes_accessed=2 << 20, transcendentals=0),
         )(slab_sizes, tau_ao)
         return pl.pallas_call(
-            functools.partial(kernel, n),
+            functools.partial(kernel, n, reps, groups),
             out_shape=jax.ShapeDtypeStruct((pairs, LANES), f32),
             in_specs=[pl.BlockSpec(memory_space=pltpu.VMEM)] + [pl.BlockSpec(memory_space=pltpu.HBM)] * 2,
             out_specs=pl.BlockSpec(memory_space=pltpu.VMEM),
@@ -245,13 +238,12 @@
                 pltpu.VMEM((slots, virtuals), bf),
                 pltpu.VMEM((slots, virtuals), bf),
                 pltpu.VMEM((n, pairs, slots), bf),
-                pltpu.VMEM((n, 2, 2, pairs, LANES), f32),
-                pltpu.VMEM((n, 2, pairs, LANES), f32),
-                pltpu.VMEM((n, pairs, LANES), f32),
+                pltpu.VMEM((reps, n, pairs, LANES), f32),
+                pltpu.VMEM((reps - 1, n, pairs, LANES), f32),
                 pltpu.VMEM((n, pairs, LANES), f32),
                 pltpu.VMEM((n, pairs, LANES), f32),
                 dma((3,)),
-            ] + [dma((n,))] * 8,
+            ] + [dma((n,))] * 2 + [dma((reps - 1, len(groups)))] * 2 + [dma((n,))] * 2,
             compiler_params=pltpu.CompilerParams(
                 collective_id=0, has_side_effects=True, vmem_limit_bytes=211 << 18
             ),

time: 32.5 us -> 33.6 us (1.034)
  Pallas kernels: 31 us -> 32.2 us
    pallas_call x1, Pallas kernels: 28.8 us -> 29.9 us  [body(): pl.pallas_call(functools.partial(kernel, n, reps, groups), out_shape=jax....]
where the time goes in v8:
time: 33.6 us; the launch traced here: 33.4 us
  Pallas kernels  32.2 us (96%)
  local copies, waits for them, and re-layouts  1.27 us (4%)
    pallas_call x1, Pallas kernels, body(): pl.pallas_call(functools.partial(kernel, n, reps, groups), out_shape=jax....  29.9 us
    pallas_call x1, Pallas kernels, body(): pl.pallas_call(functools.partial(pick_kernel, n, slabs), out_shape=jax.Sh...  2.26 us
    unnamed x3, local copies, waits for them, and re-layouts  1.27 us

profile of v8, /device:TPU:0, one launch (start us, length us, event | category | flops | bytes accessed | tf_op | source)
XLA Modules:
  0.0 33.4 jit_solution(3700031578581468345)
XLA Ops:
  0.0 0.0 copy-start
  0.0 0.7 %copy-done = s32[32]{0:T(128)S(1)} copy-done((s32[32]{0:T(128)S(1)}, s32[32]{0:T(128)}, u32[]{:S(2)}) %copy-start) | copy-done | bytes 152
  0.7 2.3 %shard_map.46.amps_out = bf16[8,64,512]{2,1,0:T(8,128)(2,1)S(1)} custom-call(s32[32]{0:T(128)S(1)} %copy-done, bf16[64,8192]{1,0:T(8,128)(2,1)} %tau_in.1), custom_call_target="tpu_custom_call" | custom-call | bytes 2097152 | tf_op jit(solution)/shard_map/pallas_call | solution.py:216
  2.9 29.9 %shard_map.47 = f32[64,128]{1,0:T(8,128)S(1)} custom-call(bf16[8,64,512]{2,1,0:T(8,128)(2,1)S(1)} %shard_map.46.amps_out, bf16[4,128,1024]{2,1,0:T(8,128)(2,1)} %integrals_in.1, f32[1024,512]{1,0:T(8,128)} %transform_in.1), custom_call_target="tpu_custom_call" | custom-call | flops 1610612736 | bytes 4194304 | tf_op jit(solution)/shard_map/pallas_call | solution.py:228
  32.8 0.6 %copy.6 = f32[64,128]{1,0:T(8,128)} copy(f32[64,128]{1,0:T(8,128)S(1)} %shard_map.47) | data formatting | bytes 65536
Async XLA Ops:
  0.0 0.7 %copy-start = (s32[32]{0:T(128)S(1)}, s32[32]{0:T(128)}, u32[]{:S(2)}) copy-start(s32[32]{0:T(128)} %sizes_in.1) | copy-start | bytes 388

commit v9 on v6

--- a/solution.py
+++ b/solution.py
@@ -53,13 +53,14 @@
 
 
 def kernel(
-    n, amps_out, integrals_in, transform_in, out,
-    integrals, transform, t_hi, t_lo, w_hi, w_lo, amps, part, core_in, x_in, done, back,
-    load_sem, amps_send, amps_recv, core_send, core_recv, x_send, x_recv, back_send, back_recv,
+    n, groups, amps_out, integrals_in, transform_in, out,
+    integrals, transform, t_hi, t_lo, w_hi, w_lo, amps, part, core_in, x_in, rep_in, done, back,
+    load_sem, amps_send, amps_recv, core_send, core_recv, x_send, x_recv, rep_send, rep_recv, back_send, back_recv,
 ):
     me, rep = lax.axis_index("pair"), lax.axis_index("rep")
     hi, lo = lax.div(rep, 2), lax.rem(rep, 2)
     near, far = hi * 2 + (1 - lo), (1 - hi) * 2 + lo
+    both = (1 - hi) * 2 + (1 - lo)
     slabs, rows, width = integrals.shape
 
     load_own = pltpu.make_async_copy(amps_out.at[0], amps.at[0], load_sem.at[0])
@@ -78,6 +79,7 @@
 
     pl.semaphore_signal(barrier, inc=1, device_id=(me, near), device_id_type=MESH)
     pl.semaphore_signal(barrier, inc=1, device_id=(me, far), device_id_type=MESH)
+    pl.semaphore_signal(barrier, inc=1, device_id=(me, both), device_id_type=MESH)
 
     def send_amps(slot):
         other = partner(me, slot, n)
@@ -101,6 +103,15 @@
             device_id=(me, far), device_id_type=MESH,
         )
 
+    def send_direct(slot, way):
+        other = (near, far, both)[way]
+        at = slot - groups[-1][0]
+        return pltpu.make_async_remote_copy(
+            src_ref=part.at[slot, lax.rem(other, 2), lax.div(other, 2)], dst_ref=rep_in.at[at, way],
+            send_sem=rep_send.at[at, way], recv_sem=rep_recv.at[at, way],
+            device_id=(me, other), device_id_type=MESH,
+        )
+
     def send_back(slot):
         owner = partner(me, slot, n)
         return pltpu.make_async_remote_copy(
@@ -109,7 +120,7 @@
             device_id=(owner, rep), device_id_type=MESH,
         )
 
-    pl.semaphore_wait(barrier, n + 1)
+    pl.semaphore_wait(barrier, n + 2)
 
     half = n // 2
 
@@ -142,7 +153,7 @@
 
     load_own.wait()
 
-    def multiply(first, last):
+    def multiply(first, last, direct):
         @pl.loop(first, last)
         def _(slot):
             @pl.when(slot >= 1)
@@ -161,7 +172,11 @@
                 p += jnp.dot(block, w_hi[:, columns], preferred_element_type=jnp.float32)
                 part[slot, 0, h] = p[:, :LANES]
                 part[slot, 1, h] = p[:, LANES:]
-            send_core(slot).start()
+            if direct:
+                for way in (1, 2, 0):
+                    send_direct(slot, way).start()
+            else:
+                send_core(slot).start()
 
     def sum_core(first, last):
         @pl.loop(first, last)
@@ -180,13 +195,24 @@
             def _():
                 send_back(slot).start()
 
-    groups = [(0, half)] + [(at, min(at + AHEAD, n)) for at in range(half, n, AHEAD)]
+    def sum_direct(first, last):
+        @pl.loop(first, last)
+        def _(slot):
+            total = part[slot, lo, hi]
+            for way in range(3):
+                send_direct(slot, way).wait_recv()
+                total = total + rep_in[slot - first, way]
+            done[slot] = total
+            send_back(slot).start()
+
     for at, group in enumerate(groups):
-        multiply(*group)
+        direct = at == len(groups) - 1
+        multiply(*group, direct)
         if at:
             sum_x(*groups[at - 1])
-        sum_core(*group)
-    sum_x(*groups[-1])
+        if not direct:
+            sum_core(*group)
+    sum_direct(*groups[-1])
 
     out[...] = done[0]
 
@@ -205,8 +231,15 @@
         def _():
             send_amps(slot).wait_send()
 
-        send_core(slot).wait_send()
-        send_x(slot).wait_send()
+        @pl.when(slot < groups[-1][0])
+        def _():
+            send_core(slot).wait_send()
+            send_x(slot).wait_send()
+
+        @pl.when(slot >= groups[-1][0])
+        def _():
+            for way in range(3):
+                send_direct(slot, way).wait_send()
 
 
 def solution(mesh):
@@ -218,6 +251,9 @@
         virtuals = transform.shape[1]
         assert reps == 4 and rows == LANES and virtuals == reps * LANES
         slots = slabs * rows
+        half = n // 2
+        groups = [(0, half)] + [(at, min(at + AHEAD, n)) for at in range(half, n, AHEAD)]
+        ending = groups[-1][1] - groups[-1][0]
         bf, f32, dma = jnp.bfloat16, jnp.float32, pltpu.SemaphoreType.DMA
         flops = 4 * slots * width * virtuals + 4 * n * pairs * slots * virtuals
         amps = pl.pallas_call(
@@ -233,7 +269,7 @@
             cost_estimate=pl.CostEstimate(flops=0, bytes_accessed=2 << 20, transcendentals=0),
         )(slab_sizes, tau_ao)
         return pl.pallas_call(
-            functools.partial(kernel, n),
+            functools.partial(kernel, n, groups),
             out_shape=jax.ShapeDtypeStruct((pairs, LANES), f32),
             in_specs=[pl.BlockSpec(memory_space=pltpu.VMEM)] + [pl.BlockSpec(memory_space=pltpu.HBM)] * 2,
             out_specs=pl.BlockSpec(memory_space=pltpu.VMEM),
@@ -248,10 +284,11 @@
                 pltpu.VMEM((n, 2, 2, pairs, LANES), f32),
                 pltpu.VMEM((n, 2, pairs, LANES), f32),
                 pltpu.VMEM((n, pairs, LANES), f32),
+                pltpu.VMEM((ending, 3, pairs, LANES), f32),
                 pltpu.VMEM((n, pairs, LANES), f32),
                 pltpu.VMEM((n, pairs, LANES), f32),
                 dma((3,)),
-            ] + [dma((n,))] * 8,
+            ] + [dma((n,))] * 6 + [dma((ending, 3))] * 2 + [dma((n,))] * 2,
             compiler_params=pltpu.CompilerParams(
                 collective_id=0, has_side_effects=True, vmem_limit_bytes=211 << 18
             ),

time: 32.5 us -> 32.3 us (level)
  no operation moved by 1% of the time
where the time goes in v9:
time: 32.3 us; the launch traced here: 32.2 us
  Pallas kernels  30.9 us (96%)
  local copies, waits for them, and re-layouts  1.27 us (4%)
    pallas_call x1, Pallas kernels, body(): pl.pallas_call(functools.partial(kernel, n, groups), out_shape=jax.ShapeD...  28.6 us
    pallas_call x1, Pallas kernels, body(): pl.pallas_call(functools.partial(pick_kernel, n, slabs), out_shape=jax.Sh...  2.26 us
    unnamed x3, local copies, waits for them, and re-layouts  1.27 us

profile of v9, /device:TPU:0, one launch (start us, length us, event | category | flops | bytes accessed | tf_op | source)
XLA Modules:
  0.0 32.2 jit_solution(9201029831676482569)
XLA Ops:
  0.0 0.0 copy-start
  0.0 0.7 %copy-done = s32[32]{0:T(128)S(1)} copy-done((s32[32]{0:T(128)S(1)}, s32[32]{0:T(128)}, u32[]{:S(2)}) %copy-start) | copy-done | bytes 152
  0.7 2.3 %shard_map.46.amps_out = bf16[8,64,512]{2,1,0:T(8,128)(2,1)S(1)} custom-call(s32[32]{0:T(128)S(1)} %copy-done, bf16[64,8192]{1,0:T(8,128)(2,1)} %tau_in.1), custom_call_target="tpu_custom_call" | custom-call | bytes 2097152 | tf_op jit(solution)/shard_map/pallas_call | solution.py:259
  2.9 28.6 %shard_map.47 = f32[64,128]{1,0:T(8,128)S(1)} custom-call(bf16[8,64,512]{2,1,0:T(8,128)(2,1)S(1)} %shard_map.46.amps_out, bf16[4,128,1024]{2,1,0:T(8,128)(2,1)} %integrals_in.1, f32[1024,512]{1,0:T(8,128)} %transform_in.1), custom_call_target="tpu_custom_call" | custom-call | flops 1610612736 | bytes 4194304 | tf_op jit(solution)/shard_map/pallas_call | solution.py:271
  31.6 0.6 %copy.6 = f32[64,128]{1,0:T(8,128)} copy(f32[64,128]{1,0:T(8,128)S(1)} %shard_map.47) | data formatting | bytes 65536
Async XLA Ops:
  0.0 0.7 %copy-start = (s32[32]{0:T(128)S(1)}, s32[32]{0:T(128)}, u32[]{:S(2)}) copy-start(s32[32]{0:T(128)} %sizes_in.1) | copy-start | bytes 388

commit v10 on v9

--- a/solution.py
+++ b/solution.py
@@ -207,10 +207,12 @@
 
     for at, group in enumerate(groups):
         direct = at == len(groups) - 1
+        if direct:
+            sum_x(*groups[at - 1])
         multiply(*group, direct)
-        if at:
-            sum_x(*groups[at - 1])
         if not direct:
+            if at:
+                sum_x(*groups[at - 1])
             sum_core(*group)
     sum_direct(*groups[-1])
 

time: 32.3 us -> 32.7 us (1.012)
  Pallas kernels: 30.9 us -> 31.3 us
    pallas_call x1, Pallas kernels: 28.6 us -> 29 us  [body(): pl.pallas_call(functools.partial(kernel, n, groups), out_shape=jax.ShapeD...]
where the time goes in v10:
time: 32.7 us; the launch traced here: 32.6 us
  Pallas kernels  31.3 us (96%)
  local copies, waits for them, and re-layouts  1.27 us (4%)
    pallas_call x1, Pallas kernels, body(): pl.pallas_call(functools.partial(kernel, n, groups), out_shape=jax.ShapeD...  29 us
    pallas_call x1, Pallas kernels, body(): pl.pallas_call(functools.partial(pick_kernel, n, slabs), out_shape=jax.Sh...  2.26 us
    unnamed x3, local copies, waits for them, and re-layouts  1.27 us

profile of v10, /device:TPU:0, one launch (start us, length us, event | category | flops | bytes accessed | tf_op | source)
XLA Modules:
  0.0 32.6 jit_solution(1984851214493218924)
XLA Ops:
  0.0 0.0 copy-start
  0.0 0.7 %copy-done = s32[32]{0:T(128)S(1)} copy-done((s32[32]{0:T(128)S(1)}, s32[32]{0:T(128)}, u32[]{:S(2)}) %copy-start) | copy-done | bytes 152
  0.7 2.3 %shard_map.46.amps_out = bf16[8,64,512]{2,1,0:T(8,128)(2,1)S(1)} custom-call(s32[32]{0:T(128)S(1)} %copy-done, bf16[64,8192]{1,0:T(8,128)(2,1)} %tau_in.1), custom_call_target="tpu_custom_call" | custom-call | bytes 2097152 | tf_op jit(solution)/shard_map/pallas_call | solution.py:261
  2.9 29.0 %shard_map.47 = f32[64,128]{1,0:T(8,128)S(1)} custom-call(bf16[8,64,512]{2,1,0:T(8,128)(2,1)S(1)} %shard_map.46.amps_out, bf16[4,128,1024]{2,1,0:T(8,128)(2,1)} %integrals_in.1, f32[1024,512]{1,0:T(8,128)} %transform_in.1), custom_call_target="tpu_custom_call" | custom-call | flops 1610612736 | bytes 4194304 | tf_op jit(solution)/shard_map/pallas_call | solution.py:273
  32.0 0.6 %copy.6 = f32[64,128]{1,0:T(8,128)} copy(f32[64,128]{1,0:T(8,128)S(1)} %shard_map.47) | data formatting | bytes 65536
Async XLA Ops:
  0.0 0.7 %copy-start = (s32[32]{0:T(128)S(1)}, s32[32]{0:T(128)}, u32[]{:S(2)}) copy-start(s32[32]{0:T(128)} %sizes_in.1) | copy-start | bytes 388

commit v11 on v10

--- a/solution.py
+++ b/solution.py
@@ -39,7 +39,7 @@
     places = lax.broadcasted_iota(jnp.int32, (pairs, rows), 1) + rep * rows
     load_tau.wait()
 
-    @pl.loop(0, n)
+    @pl.loop(0, n, unroll=4)
     def _(slot):
         dest = partner(me, slot, n)
         for q in range(slabs):
@@ -207,12 +207,16 @@
 
     for at, group in enumerate(groups):
         direct = at == len(groups) - 1
-        if direct:
+        first, last = group
+        if at and not direct:
+            multiply(first, first + 1, direct)
             sum_x(*groups[at - 1])
-        multiply(*group, direct)
-        if not direct:
+            multiply(first + 1, last, direct)
+        else:
+            multiply(first, last, direct)
             if at:
                 sum_x(*groups[at - 1])
+        if not direct:
             sum_core(*group)
     sum_direct(*groups[-1])
 

time: 32.7 us -> 31.9 us (0.976)
  Pallas kernels: 31.3 us -> 30.5 us
    pallas_call x1, Pallas kernels: 2.26 us -> 1.76 us  [body(): pl.pallas_call(functools.partial(pick_kernel, n, slabs), out_shape=jax.Sh...]
where the time goes in v11:
time: 31.9 us; the launch traced here: 31.8 us
  Pallas kernels  30.5 us (96%)
  local copies, waits for them, and re-layouts  1.27 us (4%)
    pallas_call x1, Pallas kernels, body(): pl.pallas_call(functools.partial(kernel, n, groups), out_shape=jax.ShapeD...  28.7 us
    pallas_call x1, Pallas kernels, body(): pl.pallas_call(functools.partial(pick_kernel, n, slabs), out_shape=jax.Sh...  1.76 us
    unnamed x3, local copies, waits for them, and re-layouts  1.27 us

profile of v11, /device:TPU:0, one launch (start us, length us, event | category | flops | bytes accessed | tf_op | source)
XLA Modules:
  0.0 31.8 jit_solution(12552616751031192149)
XLA Ops:
  0.0 0.0 copy-start
  0.0 0.7 %copy-done = s32[32]{0:T(128)S(1)} copy-done((s32[32]{0:T(128)S(1)}, s32[32]{0:T(128)}, u32[]{:S(2)}) %copy-start) | copy-done | bytes 152
  0.7 1.8 %shard_map.46.amps_out = bf16[8,64,512]{2,1,0:T(8,128)(2,1)S(1)} custom-call(s32[32]{0:T(128)S(1)} %copy-done, bf16[64,8192]{1,0:T(8,128)(2,1)} %tau_in.1), custom_call_target="tpu_custom_call" | custom-call | bytes 2097152 | tf_op jit(solution)/shard_map/pallas_call | solution.py:265
  2.4 28.7 %shard_map.47 = f32[64,128]{1,0:T(8,128)S(1)} custom-call(bf16[8,64,512]{2,1,0:T(8,128)(2,1)S(1)} %shard_map.46.amps_out, bf16[4,128,1024]{2,1,0:T(8,128)(2,1)} %integrals_in.1, f32[1024,512]{1,0:T(8,128)} %transform_in.1), custom_call_target="tpu_custom_call" | custom-call | flops 1610612736 | bytes 4194304 | tf_op jit(solution)/shard_map/pallas_call | solution.py:277
  31.2 0.6 %copy.6 = f32[64,128]{1,0:T(8,128)} copy(f32[64,128]{1,0:T(8,128)S(1)} %shard_map.47) | data formatting | bytes 65536
Async XLA Ops:
  0.0 0.7 %copy-start = (s32[32]{0:T(128)S(1)}, s32[32]{0:T(128)}, u32[]{:S(2)}) copy-start(s32[32]{0:T(128)} %sizes_in.1) | copy-start | bytes 388

commit v12 on v11

--- a/solution.py
+++ b/solution.py
@@ -154,7 +154,7 @@
     load_own.wait()
 
     def multiply(first, last, direct):
-        @pl.loop(first, last)
+        @pl.loop(first, last, unroll=2 - (last - first) % 2)
         def _(slot):
             @pl.when(slot >= 1)
             def _():
@@ -179,14 +179,14 @@
                 send_core(slot).start()
 
     def sum_core(first, last):
-        @pl.loop(first, last)
+        @pl.loop(first, last, unroll=2 - (last - first) % 2)
         def _(slot):
             send_core(slot).wait_recv()
             part[slot, lo, 1 - hi] = part[slot, lo, 1 - hi] + core_in[slot, 1 - hi]
             send_x(slot).start()
 
     def sum_x(first, last):
-        @pl.loop(first, last)
+        @pl.loop(first, last, unroll=2 - (last - first) % 2)
         def _(slot):
             send_x(slot).wait_recv()
             done[slot] = part[slot, lo, hi] + core_in[slot, hi] + x_in[slot]
@@ -196,7 +196,7 @@
                 send_back(slot).start()
 
     def sum_direct(first, last):
-        @pl.loop(first, last)
+        @pl.loop(first, last, unroll=2 - (last - first) % 2)
         def _(slot):
             total = part[slot, lo, hi]
             for way in range(3):

time: 31.9 us -> 31.9 us (level)
  no operation moved by 1% of the time
where the time goes in v12:
time: 31.9 us; the launch traced here: 31.8 us
  Pallas kernels  30.5 us (96%)
  local copies, waits for them, and re-layouts  1.27 us (4%)
    pallas_call x1, Pallas kernels, body(): pl.pallas_call(functools.partial(kernel, n, groups), out_shape=jax.ShapeD...  28.7 us
    pallas_call x1, Pallas kernels, body(): pl.pallas_call(functools.partial(pick_kernel, n, slabs), out_shape=jax.Sh...  1.76 us
    unnamed x3, local copies, waits for them, and re-layouts  1.27 us

profile of v12, /device:TPU:0, one launch (start us, length us, event | category | flops | bytes accessed | tf_op | source)
XLA Modules:
  0.0 31.8 jit_solution(6318558905768829823)
XLA Ops:
  0.0 0.0 copy-start
  0.0 0.7 %copy-done = s32[32]{0:T(128)S(1)} copy-done((s32[32]{0:T(128)S(1)}, s32[32]{0:T(128)}, u32[]{:S(2)}) %copy-start) | copy-done | bytes 152
  0.7 1.8 %shard_map.46.amps_out = bf16[8,64,512]{2,1,0:T(8,128)(2,1)S(1)} custom-call(s32[32]{0:T(128)S(1)} %copy-done, bf16[64,8192]{1,0:T(8,128)(2,1)} %tau_in.1), custom_call_target="tpu_custom_call" | custom-call | bytes 2097152 | tf_op jit(solution)/shard_map/pallas_call | solution.py:265
  2.4 28.7 %shard_map.47 = f32[64,128]{1,0:T(8,128)S(1)} custom-call(bf16[8,64,512]{2,1,0:T(8,128)(2,1)S(1)} %shard_map.46.amps_out, bf16[4,128,1024]{2,1,0:T(8,128)(2,1)} %integrals_in.1, f32[1024,512]{1,0:T(8,128)} %transform_in.1), custom_call_target="tpu_custom_call" | custom-call | flops 1610612736 | bytes 4194304 | tf_op jit(solution)/shard_map/pallas_call | solution.py:277
  31.2 0.6 %copy.6 = f32[64,128]{1,0:T(8,128)} copy(f32[64,128]{1,0:T(8,128)S(1)} %shard_map.47) | data formatting | bytes 65536
Async XLA Ops:
  0.0 0.7 %copy-start = (s32[32]{0:T(128)S(1)}, s32[32]{0:T(128)}, u32[]{:S(2)}) copy-start(s32[32]{0:T(128)} %sizes_in.1) | copy-start | bytes 388
